TPU v7x, 32 devices: a whole 2x2x4 slice. The times are simulated.
32 devices in a mesh: row: 4 (over x, core), circ: 8 (over z, y).
Axes of the slice: x: 2, y: 2, z: 4, core: 2. Of those that a mesh axis runs over, the one named last changes fastest.
Arguments:
- flow_state: float32 [5, 64, 32, 1024], P(None, 'row', None, 'circ'), may hold values from -4 to 4
- velocity: float32 [3, 64, 32, 1024], P(None, 'row', None, 'circ'), may hold values from -3 to 3
- offsets: int32 [3, 3], replicated, may hold values from 0 to 1023, as said below
- passage_shift: int32 [4], replicated, may hold values from 0 to 7, as said below
- donor_step: int32 [4, 2, 1024], P('row', None, 'circ'), may hold values from 0 to 127
- donor_weight: float32 [4, 2, 1024], P('row', None, 'circ'), may hold values from 0.05 to 0.95
Outputs:
- updated_state: float32 [5, 64, 32, 1024], P(None, 'row', None, 'circ')
Inputs may be any that keep to these rules, and one draw needn't show every extreme that they name: Rotation offsets in cells; some interface takes the offset 1024 - 1 at some section in every draw, and with two or more interfaces some takes 0. `passage_shift`: passage index placed on device column 0 of each row; some row has 8 - 1 and some row 0 in every draw.
All inputs are finite; a program needn't handle non-finite values.
Results may differ from a plain program's by a relative error of at most 0.0003.
Values sent between devices are 32-bit elements; how exact they have to be, the bound alone decides.
A program may use at most 128 MiB of HBM per device.

v0:
```python
import jax
import jax.numpy as jnp
from jax import lax
from jax.sharding import PartitionSpec as P

SMAG_COEF = 0.1
TIME_STEP = 0.25


def passed_along(value, axis, steps):
    count = lax.axis_size(axis)
    first, last = (max(0, -steps), min(count, count - steps))
    return lax.ppermute(value, axis, [(source, source + steps) for source in range(first, last)])


def extended(cells, sides, width):
    for axis, dim in sides:
        count = lax.axis_size(axis)
        head = lax.slice_in_dim(cells, 0, width, axis=dim)
        tail = lax.slice_in_dim(cells, cells.shape[dim] - width, cells.shape[dim], axis=dim)
        cells = jnp.concatenate(
            [
                lax.ppermute(tail, axis, [(i, (i + 1) % count) for i in range(count)]),
                cells,
                lax.ppermute(head, axis, [((i + 1) % count, i) for i in range(count)]),
            ],
            axis=dim,
        )
    return cells


def combine(fields, axial_ext, radial_ext, around_ext, velocity):
    d_axial = 0.5 * (axial_ext[:, 2:] - axial_ext[:, :-2])
    d_radial = 0.5 * (radial_ext[:, :, 2:] - radial_ext[:, :, :-2])
    d_around = 0.5 * (around_ext[..., 2:] - around_ext[..., :-2])
    laplace = (
        axial_ext[:, 2:]
        + axial_ext[:, :-2]
        + radial_ext[:, :, 2:]
        + radial_ext[:, :, :-2]
        + around_ext[..., 2:]
        + around_ext[..., :-2]
        - 6.0 * fields
    )
    strain = jnp.sum(d_axial[1:4] ** 2 + d_radial[1:4] ** 2 + d_around[1:4] ** 2, axis=0)
    eddy_visc = SMAG_COEF * jnp.sqrt(strain + 1.0)
    return eddy_visc * laplace - (
        velocity[0] * d_axial + velocity[1] * d_radial + velocity[2] * d_around
    )


def radial_pad(fields):
    return jnp.concatenate([fields[:, :, :1], fields, fields[:, :, -1:]], axis=2)


def axial_pad(fields, lower_ghost, upper_ghost):
    return jnp.concatenate([lower_ghost[:, None], fields, upper_ghost[:, None]], axis=1)


def local(flow_state, velocity, offsets, passage_shift, donor_step, donor_weight):
    row_count = lax.axis_size("row")
    loop_size = lax.axis_size("circ")
    row_id = lax.axis_index("row")
    column = lax.axis_index("circ")
    pitch_cells = flow_state.shape[-1]
    loop_cells = pitch_cells * loop_size
    passage = (column - passage_shift[row_id]) % loop_size
    lower_src = jnp.maximum(row_id - 1, 0)
    upper_src = jnp.minimum(row_id + 1, row_count - 1)
    lower_face = jnp.maximum(row_id - 1, 0)
    upper_face = jnp.minimum(row_id, row_count - 2)
    within = jnp.arange(pitch_cells, dtype=jnp.int32)

    def interface(face_plane, source_row, offset, donor_steps, weights):
        gathered = lax.all_gather(face_plane, "circ", axis=2, tiled=True)
        ordered = jnp.roll(gathered, -passage_shift[source_row] * pitch_cells, axis=2)
        donor_cols = (passage * pitch_cells + within + offset + donor_steps) % loop_cells
        next_cols = (donor_cols + 1) % loop_cells
        return weights * jnp.take(ordered, donor_cols, axis=2) + (1.0 - weights) * jnp.take(
            ordered, next_cols, axis=2
        )

    def evaluate(fields, section_index):
        first_plane = fields[:, 0]
        last_plane = fields[:, -1]
        from_below = passed_along(last_plane, "row", 1)
        from_above = passed_along(first_plane, "row", -1)
        low_offset = offsets[section_index, lower_face]
        high_offset = (loop_cells - offsets[section_index, upper_face]) % loop_cells
        lower_ghost = interface(
            from_below, lower_src, low_offset, donor_step[0, 0], donor_weight[0, 0]
        )
        upper_ghost = interface(
            from_above, upper_src, high_offset, donor_step[0, 1], donor_weight[0, 1]
        )
        lower_ghost = jnp.where(row_id == 0, first_plane, lower_ghost)
        upper_ghost = jnp.where(row_id == row_count - 1, last_plane, upper_ghost)
        around_ext = extended(fields, (("circ", 3),), 1)
        return combine(
            fields,
            axial_pad(fields, lower_ghost, upper_ghost),
            radial_pad(fields),
            around_ext,
            velocity,
        )

    section_one = flow_state + TIME_STEP * evaluate(flow_state, 0)
    section_two = 0.75 * flow_state + 0.25 * (section_one + TIME_STEP * evaluate(section_one, 1))
    return 1.0 / 3.0 * flow_state + 2.0 / 3.0 * (section_two + TIME_STEP * evaluate(section_two, 2))


def solution(mesh):
    placed = (
        P(None, "row", None, "circ"),
        P(None, "row", None, "circ"),
        P(),
        P(),
        P("row", None, "circ"),
        P("row", None, "circ"),
    )
    return jax.shard_map(
        local, mesh=mesh, in_specs=placed, out_specs=P(None, "row", None, "circ"), check_vma=False
    )
```

profile of v0, /device:TPU:2, one launch (start us, length us, event | category | flops | bytes accessed | tf_op | source)
XLA Modules:
  0.0 394.2 jit_solution(9017633646635376605)
XLA Ops:
  11.8 4.6 %collective-permute-start.2 = (f32[5,16,32,1]{2,1,3,0:T(8,128)S(1)}, f32[5,16,32,1]{2,1,3,0:T(8,128)}, u32[]{:S(2)}, u32[]{:S(2)}) collective-permute-start(f32[5,16,32,1]{2,1,3,0:T(8,128)S(1)} %copy.304), channel_id=1, source_target_pairs={{1,0},{2,1},{3,2},{4,3},{5,4},{6,5},{7,6},{0,7},{9,8},{10,9},{11,1... | collective-permute-start | bytes 30728 | tf_op jit(solution)/shard_map/ppermute | solution.py:25
  38.1 32.0 %all_gather.18 = f32[5,32,1024]{2,1,0:T(8,128)S(1)} all-gather(f32[5,32,128]{2,1,0:T(8,128)} %collective-permute-done), channel_id=1, replica_groups=mesh['row'=4,'circ'=8] {'circ'}, dimensions={2}, use_global_device_ids=true | all-gather | bytes 737280 | tf_op jit(solution)/shard_map/all_gather | solution.py:75
  71.4 3.6 copy.302
  74.9 3.8 gather_fusion.1
  80.5 3.8 gather_fusion
  86.1 31.7 %all_gather.19 = f32[5,32,1024]{2,1,0:T(8,128)S(1)} all-gather(f32[5,32,128]{2,1,0:T(8,128)} %collective-permute-done.1), channel_id=1, replica_groups=mesh['row'=4,'circ'=8] {'circ'}, dimensions={2}, use_global_device_ids=true | all-gather | bytes 737280 | tf_op jit(solution)/shard_map/all_gather | solution.py:75
  119.1 3.6 copy.303
  122.7 3.8 gather_fusion.2
  128.2 3.8 gather_fusion.3
  147.8 4.5 %collective-permute-start.6 = (f32[5,16,32,1]{2,1,3,0:T(8,128)S(1)}, f32[5,16,32,1]{2,1,3,0:T(8,128)}, u32[]{:S(2)}, u32[]{:S(2)}) collective-permute-start(f32[5,16,32,1]{2,1,3,0:T(8,128)S(1)} %copy.282), channel_id=1, source_target_pairs={{1,0},{2,1},{3,2},{4,3},{5,4},{6,5},{7,6},{0,7},{9,8},{10,9},{11,1... | collective-permute-start | bytes 30728 | tf_op jit(solution)/shard_map/ppermute | solution.py:25
  164.4 32.1 %all_gather.20 = f32[5,32,1024]{2,1,0:T(8,128)S(1)} all-gather(f32[5,32,128]{2,1,0:T(8,128)} %collective-permute-done.4), channel_id=1, replica_groups=mesh['row'=4,'circ'=8] {'circ'}, dimensions={2}, use_global_device_ids=true | all-gather | bytes 737280 | tf_op jit(solution)/shard_map/all_gather | solution.py:75
  197.8 3.6 copy.308
  201.4 3.8 gather_fusion.5
  206.9 3.8 gather_fusion.4
  212.5 31.9 %all_gather.21 = f32[5,32,1024]{2,1,0:T(8,128)S(1)} all-gather(f32[5,32,128]{2,1,0:T(8,128)} %collective-permute-done.5), channel_id=1, replica_groups=mesh['row'=4,'circ'=8] {'circ'}, dimensions={2}, use_global_device_ids=true | all-gather | bytes 737280 | tf_op jit(solution)/shard_map/all_gather | solution.py:75
  245.7 3.6 copy.309
  249.3 3.8 gather_fusion.6
  254.9 3.8 gather_fusion.7
  289.6 32.0 %all_gather.22 = f32[5,32,1024]{2,1,0:T(8,128)S(1)} all-gather(f32[5,32,128]{2,1,0:T(8,128)} %collective-permute-done.8), channel_id=1, replica_groups=mesh['row'=4,'circ'=8] {'circ'}, dimensions={2}, use_global_device_ids=true | all-gather | bytes 737280 | tf_op jit(solution)/shard_map/all_gather | solution.py:75
  326.4 3.8 gather_fusion.9
  332.0 3.8 gather_fusion.8
  337.6 32.1 %all_gather.23 = f32[5,32,1024]{2,1,0:T(8,128)S(1)} all-gather(f32[5,32,128]{2,1,0:T(8,128)} %collective-permute-done.9), channel_id=1, replica_groups=mesh['row'=4,'circ'=8] {'circ'}, dimensions={2}, use_global_device_ids=true | all-gather | bytes 737280 | tf_op jit(solution)/shard_map/all_gather | solution.py:75
  374.5 3.6 gather_fusion.10
  380.0 3.6 gather_fusion.11
  (156 shorter events, 129.9 us)
Async XLA Ops:
  1.6 36.5 %collective-permute-start = (f32[5,32,128]{2,1,0:T(8,128)}, f32[5,32,128]{2,1,0:T(8,128)}, u32[]{:S(2)}, u32[]{:S(2)}) collective-permute-start(f32[5,32,128]{2,1,0:T(8,128)} %get-tuple-element.61), channel_id=1, source_target_pairs={{8,0},{16,8},{24,16},{9,1},{17,9},{25,17},{10,2},{18,10},{26,18},{... | collective-permute-start | bytes 245768 | tf_op jit(solution)/shard_map/ppermute | solution.py:13
  3.5 82.6 %collective-permute-start.1 = (f32[5,32,128]{2,1,0:T(8,128)}, f32[5,32,128]{2,1,0:T(8,128)}, u32[]{:S(2)}, u32[]{:S(2)}) collective-permute-start(f32[5,32,128]{2,1,0:T(8,128)} %get-tuple-element.60), channel_id=1, source_target_pairs={{0,8},{8,16},{16,24},{1,9},{9,17},{17,25},{2,10},{10,18},{18,26},{... | collective-permute-start | bytes 245768 | tf_op jit(solution)/shard_map/ppermute | solution.py:13
  9.8 11.7 %copy-start.25 = (s32[1,2,128]{2,1,0:T(2,128)S(1)}, s32[1,2,128]{2,1,0:T(2,128)}, u32[]{:S(2)}) copy-start(s32[1,2,128]{2,1,0:T(2,128)} %param.14) | copy-start | bytes 3076
  9.8 14.8 %copy-start = (f32[5,16,32,128]{3,2,1,0:T(8,128)S(1)}, f32[5,16,32,128]{3,2,1,0:T(8,128)}, u32[]{:S(2)}) copy-start(f32[5,16,32,128]{3,2,1,0:T(8,128)} %param.10) | copy-start | bytes 3932164
  9.9 18.4 %copy-start.24 = (f32[1,2,128]{2,1,0:T(2,128)S(1)}, f32[1,2,128]{2,1,0:T(2,128)}, u32[]{:S(2)}) copy-start(f32[1,2,128]{2,1,0:T(2,128)} %param.15) | copy-start | bytes 3076
  11.8 22.5 %collective-permute-start.2 = (f32[5,16,32,1]{2,1,3,0:T(8,128)S(1)}, f32[5,16,32,1]{2,1,3,0:T(8,128)}, u32[]{:S(2)}, u32[]{:S(2)}) collective-permute-start(f32[5,16,32,1]{2,1,3,0:T(8,128)S(1)} %copy.304), channel_id=1, source_target_pairs={{1,0},{2,1},{3,2},{4,3},{5,4},{6,5},{7,6},{0,7},{9,8},{10,9},{11,1... | collective-permute-start | bytes 30728 | tf_op jit(solution)/shard_map/ppermute | solution.py:25
  17.6 18.1 %collective-permute-start.3 = (f32[5,16,32,1]{2,1,3,0:T(8,128)}, f32[5,16,32,1]{2,1,3,0:T(8,128)}, u32[]{:S(2)}, u32[]{:S(2)}) collective-permute-start(f32[5,16,32,1]{2,1,3,0:T(8,128)} %copy.305), channel_id=1, source_target_pairs={{0,1},{1,2},{2,3},{3,4},{4,5},{5,6},{6,7},{7,0},{8,9},{9,10},{10,1... | collective-permute-start | bytes 30728 | tf_op jit(solution)/shard_map/ppermute | solution.py:23
  35.6 99.3 %copy-start.3 = (f32[5,16,32,1]{3,2,1,0:T(8,128)}, f32[5,16,32,1]{3,2,1,0:T(8,128)S(1)}, u32[]{:S(2)}) copy-start(f32[5,16,32,1]{3,2,1,0:T(8,128)S(1)} %copy.269) | copy-start | bytes 30724
  122.6 11.2 %copy-start.16 = (pred[128]{0:T(512)(128)(4,1)S(1)}, pred[128]{0:T(512)(128)(4,1)}, u32[]{:S(2)}) copy-start(pred[128]{0:T(512)(128)(4,1)} %get-tuple-element.25) | copy-start | bytes 388
  122.6 11.2 %copy-start.17 = (pred[128]{0:T(512)(128)(4,1)S(1)}, pred[128]{0:T(512)(128)(4,1)}, u32[]{:S(2)}) copy-start(pred[128]{0:T(512)(128)(4,1)} %get-tuple-element.94) | copy-start | bytes 388
  122.6 11.2 %copy-start.22 = (pred[128]{0:T(512)(128)(4,1)S(1)}, pred[128]{0:T(512)(128)(4,1)}, u32[]{:S(2)}) copy-start(pred[128]{0:T(512)(128)(4,1)} %get-tuple-element.79) | copy-start | bytes 388
  122.6 11.2 %copy-start.23 = (pred[128]{0:T(512)(128)(4,1)S(1)}, pred[128]{0:T(512)(128)(4,1)}, u32[]{:S(2)}) copy-start(pred[128]{0:T(512)(128)(4,1)} %get-tuple-element.81) | copy-start | bytes 388
  141.3 120.3 %copy-start.1 = (f32[5,16,32,128]{3,2,1,0:T(8,128)}, f32[5,16,32,128]{3,2,1,0:T(8,128)S(1)}, u32[]{:S(2)}) copy-start(f32[5,16,32,128]{3,2,1,0:T(8,128)S(1)} %multiply_add_fusion.2) | copy-start | bytes 3932164
  144.0 20.4 %collective-permute-start.4 = (f32[5,32,128]{2,1,0:T(8,128)}, f32[5,32,128]{2,1,0:T(8,128)}, u32[]{:S(2)}, u32[]{:S(2)}) collective-permute-start(f32[5,32,128]{2,1,0:T(8,128)} %get-tuple-element.50), channel_id=1, source_target_pairs={{8,0},{16,8},{24,16},{9,1},{17,9},{25,17},{10,2},{18,10},{26,18},{... | collective-permute-start | bytes 245768 | tf_op jit(solution)/shard_map/ppermute | solution.py:13
  147.8 9.7 %collective-permute-start.6 = (f32[5,16,32,1]{2,1,3,0:T(8,128)S(1)}, f32[5,16,32,1]{2,1,3,0:T(8,128)}, u32[]{:S(2)}, u32[]{:S(2)}) collective-permute-start(f32[5,16,32,1]{2,1,3,0:T(8,128)S(1)} %copy.282), channel_id=1, source_target_pairs={{1,0},{2,1},{3,2},{4,3},{5,4},{6,5},{7,6},{0,7},{9,8},{10,9},{11,1... | collective-permute-start | bytes 30728 | tf_op jit(solution)/shard_map/ppermute | solution.py:25
  154.7 7.3 %collective-permute-start.7 = (f32[5,16,32,1]{2,1,3,0:T(8,128)}, f32[5,16,32,1]{2,1,3,0:T(8,128)}, u32[]{:S(2)}, u32[]{:S(2)}) collective-permute-start(f32[5,16,32,1]{2,1,3,0:T(8,128)} %copy.284), channel_id=1, source_target_pairs={{0,1},{1,2},{2,3},{3,4},{4,5},{5,6},{6,7},{7,0},{8,9},{9,10},{10,1... | collective-permute-start | bytes 30728 | tf_op jit(solution)/shard_map/ppermute | solution.py:23
  154.7 57.8 %collective-permute-start.5 = (f32[5,32,128]{2,1,0:T(8,128)}, f32[5,32,128]{2,1,0:T(8,128)}, u32[]{:S(2)}, u32[]{:S(2)}) collective-permute-start(f32[5,32,128]{2,1,0:T(8,128)} %get-tuple-element.49), channel_id=1, source_target_pairs={{0,8},{8,16},{16,24},{1,9},{9,17},{17,25},{2,10},{10,18},{18,26},{... | collective-permute-start | bytes 245768 | tf_op jit(solution)/shard_map/ppermute | solution.py:13
  249.3 11.2 %copy-start.15 = (pred[128]{0:T(512)(128)(4,1)S(1)}, pred[128]{0:T(512)(128)(4,1)}, u32[]{:S(2)}) copy-start(pred[128]{0:T(512)(128)(4,1)} %get-tuple-element.92) | copy-start | bytes 388
  249.3 11.2 %copy-start.20 = (pred[128]{0:T(512)(128)(4,1)S(1)}, pred[128]{0:T(512)(128)(4,1)}, u32[]{:S(2)}) copy-start(pred[128]{0:T(512)(128)(4,1)} %get-tuple-element.75) | copy-start | bytes 388
  249.3 11.2 %copy-start.21 = (pred[128]{0:T(512)(128)(4,1)S(1)}, pred[128]{0:T(512)(128)(4,1)}, u32[]{:S(2)}) copy-start(pred[128]{0:T(512)(128)(4,1)} %get-tuple-element.77) | copy-start | bytes 388
  271.2 18.4 %collective-permute-start.8 = (f32[5,32,128]{2,1,0:T(8,128)}, f32[5,32,128]{2,1,0:T(8,128)}, u32[]{:S(2)}, u32[]{:S(2)}) collective-permute-start(f32[5,32,128]{2,1,0:T(8,128)} %get-tuple-element.39), channel_id=1, source_target_pairs={{8,0},{16,8},{24,16},{9,1},{17,9},{25,17},{10,2},{18,10},{26,18},{... | collective-permute-start | bytes 245768 | tf_op jit(solution)/shard_map/ppermute | solution.py:13
  274.9 7.8 %collective-permute-start.10 = (f32[5,16,32,1]{2,1,3,0:T(8,128)S(1)}, f32[5,16,32,1]{2,1,3,0:T(8,128)}, u32[]{:S(2)}, u32[]{:S(2)}) collective-permute-start(f32[5,16,32,1]{2,1,3,0:T(8,128)S(1)} %copy.296), channel_id=1, source_target_pairs={{1,0},{2,1},{3,2},{4,3},{5,4},{6,5},{7,6},{0,7},{9,8},{10,9},{11,1... | collective-permute-start | bytes 30728 | tf_op jit(solution)/shard_map/ppermute | solution.py:25
  279.9 7.3 %collective-permute-start.11 = (f32[5,16,32,1]{2,1,3,0:T(8,128)}, f32[5,16,32,1]{2,1,3,0:T(8,128)}, u32[]{:S(2)}, u32[]{:S(2)}) collective-permute-start(f32[5,16,32,1]{2,1,3,0:T(8,128)} %copy.298), channel_id=1, source_target_pairs={{0,1},{1,2},{2,3},{3,4},{4,5},{5,6},{6,7},{7,0},{8,9},{9,10},{10,1... | collective-permute-start | bytes 30728 | tf_op jit(solution)/shard_map/ppermute | solution.py:23
  280.0 57.6 %collective-permute-start.9 = (f32[5,32,128]{2,1,0:T(8,128)}, f32[5,32,128]{2,1,0:T(8,128)}, u32[]{:S(2)}, u32[]{:S(2)}) collective-permute-start(f32[5,32,128]{2,1,0:T(8,128)} %get-tuple-element.38), channel_id=1, source_target_pairs={{0,8},{8,16},{16,24},{1,9},{9,17},{17,25},{2,10},{10,18},{18,26},{... | collective-permute-start | bytes 245768 | tf_op jit(solution)/shard_map/ppermute | solution.py:13
  (14 other events, 84.5 us)
where the time goes:
time: 398 us; the launch traced here: 394 us
  blocking collectives  192 us (48%)
  local copies, waits for them, and re-layouts  129 us (32%)
  other arithmetic  39.2 us (10%)
  starting transfers between devices  25.8 us (6%)
  between operations  4.32 us (1%)
  waiting for transfers between devices  4.18 us (1%)
    all_gather x6, blocking collectives, interface(): gathered = lax.all_gather(face_plane, 'circ', axis=2, tiled=True)  192 us
    gather x12, local copies, waits for them, and re-layouts, interface(): jnp.take(ordered, donor_cols, axis=2)  33.4 us
    gather x12, local copies, waits for them, and re-layouts, interface(): jnp.take(ordered, next_cols, axis=2)  33.4 us
    unnamed x60, local copies, waits for them, and re-layouts  28.5 us
    ppermute x6, starting transfers between devices, passed_along(): lax.ppermute(value, axis, [(source, source + steps) for source in range(f...  14.3 us
    slice x5, local copies, waits for them, and re-layouts, extended(): lax.slice_in_dim(cells, cells.shape[dim] - width, cells.shape[dim], axis=...  12.1 us
    ppermute x3, starting transfers between devices, extended(): lax.ppermute(head, axis, [((i + 1) % count, i) for i in range(count)])  11.5 us
    sub x3, other arithmetic, combine(): d_axial = 0.5 * (axial_ext[:, 2:] - axial_ext[:, :-2])  9.27 us
  transfers between devices with their start and end apart: 12, of which 2 were waited for; matrix products, arithmetic and copies ran while one was open for 23% of the time, Pallas kernels for 0%

commit v1 on v0

v1 whole, which is shorter than its diff:
```python
import functools

import jax
import jax.numpy as jnp
from jax import lax
from jax.experimental import pallas as pl
from jax.experimental.pallas import tpu as pltpu
from jax.sharding import PartitionSpec as P

SMAG_COEF = 0.1
TIME_STEP = 0.25
SECTIONS = 3
LANES = 128
GROUP = 8


def kernel(
    row_count, count,
    q_ref, u_ref, off_ref, shift_ref, step_ref, weight_ref, out_ref,
    v1, v2, pack, halo, comb, sel, ghost,
    send_sem, fwd_sem, recv_sem, halo_send, halo_recv, *slots
):
    comps, planes, radial, cells = q_ref.shape
    groups = radial // GROUP
    half = count // 2
    loop_cells = count * cells
    row = lax.axis_index("row")
    col = lax.axis_index("circ")
    odd = lax.rem(col, 2)
    partner = col + 1 - 2 * odd
    right = lax.rem(col + 1, count)
    left = lax.rem(col + count - 1, count)
    has = (row > 0, row < row_count - 1)
    other_row = (row - 1, row + 1)
    fields = (q_ref, v1, v2, out_ref)
    order = sorted(range(half), key=lambda d: (min(d, half - d), d))

    lane = lax.broadcasted_iota(jnp.int32, (radial, cells), 1)
    line = lax.broadcasted_iota(jnp.int32, (radial, cells), 0)
    lane8 = lax.broadcasted_iota(jnp.int32, (GROUP, cells), 1)
    is_first, is_last = lane == 0, lane == cells - 1
    is_inner, is_outer = line == 0, line == radial - 1

    def away(d):
        return lax.rem(col + 2 * d, count)

    def back(d):
        return lax.rem(col + count - 2 * d, count)

    def across(d):
        return lax.rem(partner + count - 2 * d, count)

    def face_copy(s, face, d):
        plane = planes - 1 if face == 0 else 0
        return pltpu.make_async_remote_copy(
            src_ref=fields[s].at[:, plane],
            dst_ref=slots[2 * s + face].at[col],
            send_sem=send_sem.at[s, face, d],
            recv_sem=recv_sem.at[s, face, col],
            device_id={"row": other_row[1 - face], "circ": away(d)},
            device_id_type=pl.DeviceIdType.MESH,
        )

    def forward_copy(s, face, d):
        return pltpu.make_async_remote_copy(
            src_ref=slots[2 * s + face].at[back(d)],
            dst_ref=slots[2 * s + face].at[back(d)],
            send_sem=fwd_sem.at[s, face, d],
            recv_sem=recv_sem.at[s, face, back(d)],
            device_id={"row": row, "circ": partner},
            device_id_type=pl.DeviceIdType.MESH,
        )

    def arrival(s, face, slot):
        return pltpu.make_async_remote_copy(
            src_ref=slots[2 * s + face].at[slot],
            dst_ref=slots[2 * s + face].at[slot],
            send_sem=fwd_sem.at[s, face, 0],
            recv_sem=recv_sem.at[s, face, slot],
            device_id={"row": row, "circ": partner},
            device_id_type=pl.DeviceIdType.MESH,
        )

    def halo_copy(s, side):
        return pltpu.make_async_remote_copy(
            src_ref=pack.at[s],
            dst_ref=halo.at[s, side],
            send_sem=halo_send.at[s, side],
            recv_sem=halo_recv.at[s, side],
            device_id={"row": row, "circ": right if side == 0 else left},
            device_id_type=pl.DeviceIdType.MESH,
        )

    def send_face(s, face):
        @pl.when(has[1 - face])
        def _():
            for d in order:
                face_copy(s, face, d).start()

    def send_halo(s):
        halo_copy(s, 0).start()
        halo_copy(s, 1).start()

    def forward(s, d):
        for face in (0, 1):
            @pl.when(has[face])
            def _():
                arrival(s, face, back(d)).wait_recv()
                forward_copy(s, face, d).start()

    def put_ends(s, m, a, value):
        packed = pack[s, m]
        for g in range(groups):
            spot = 2 * (a * groups + g)
            here = jnp.bitwise_and(lane8 + 1 - spot, cells - 1) < 2
            moved = pltpu.roll(value[g * GROUP:(g + 1) * GROUP], spot, 1)
            packed = jnp.where(here, moved, packed)
        pack[s, m] = packed

    def donor_base(s, face):
        source = jnp.clip(other_row[face], 0, row_count - 1)
        at = jnp.clip(row - 1 + face, 0, row_count - 2)
        offset = off_ref[s, at]
        offset = offset if face == 0 else lax.rem(loop_cells - offset, loop_cells)
        passage = col - shift_ref[row] + shift_ref[source] + offset // cells + 2 * count
        return passage, lax.rem(offset, cells)

    def build_select(s):
        spots = lax.broadcasted_iota(jnp.int32, (3 * cells, cells), 0)
        within = lax.broadcasted_iota(jnp.int32, (1, cells), 1)
        for face in (0, 1):
            _, start = donor_base(s, face)
            donor = within + start + step_ref[0, face:face + 1, :]
            for nxt in (0, 1):
                hot = jnp.where(spots == donor + nxt, 1.0, 0.0).astype(jnp.bfloat16)
                sel[face, :, nxt * cells:(nxt + 1) * cells] = hot

    def make_ghost(s, face):
        @pl.when(has[face])
        def _():
            passage, _ = donor_base(s, face)
            total = None
            for k in range(3):
                block = slots[2 * s + face][lax.rem(passage + k, count)].reshape(comps * radial, cells)
                high = block.astype(jnp.bfloat16)
                low = (block - high.astype(jnp.float32)).astype(jnp.bfloat16)
                part = sel[face, k * cells:(k + 1) * cells, :]
                for piece in (high, low):
                    got = jnp.dot(piece, part, preferred_element_type=jnp.float32)
                    total = got if total is None else total + got
            weight = weight_ref[0, face:face + 1, :]
            value = weight * total[:, :cells] + (1.0 - weight) * total[:, cells:]
            ghost[face] = value.reshape(comps, radial, cells)

        @pl.when(jnp.logical_not(has[face]))
        def _():
            ghost[face] = fields[s][:, 0 if face == 0 else planes - 1]

    def update(s, a, lower, upper):
        src, dst = fields[s], fields[s + 1]
        u_ax, u_rad, u_circ = 0.5 * u_ref[0, a], 0.5 * u_ref[1, a], 0.5 * u_ref[2, a]

        def terms(m):
            v, lo, hi = src[m, a], lower(m), upper(m)
            inner = jnp.where(is_inner, v, pltpu.roll(v, 1, 0))
            outer = jnp.where(is_outer, v, pltpu.roll(v, radial - 1, 0))
            edge = comb[m]
            ends = jnp.concatenate(
                [
                    pltpu.roll(edge, jnp.bitwise_and(2 * cells - 2 * (a * groups + g), cells - 1), 1)
                    for g in range(groups)
                ],
                axis=0,
            )
            before = pltpu.roll(jnp.where(is_last, ends, v), 1, 1)
            after = pltpu.roll(jnp.where(is_first, ends, v), cells - 1, 1)
            d_ax, d_rad, d_circ = hi - lo, outer - inner, after - before
            lap = ((hi + lo) + (outer + inner)) + ((after + before) - 6.0 * v)
            adv = u_ax * d_ax + u_rad * d_rad + u_circ * d_circ
            return v, d_ax, d_rad, d_circ, lap, adv

        def finish(m, v, lap, adv, nu):
            rate = nu * lap - adv
            if s == 0:
                new = v + TIME_STEP * rate
            elif s == 1:
                new = 0.75 * q_ref[m, a] + 0.25 * (v + TIME_STEP * rate)
            else:
                new = (1.0 / 3.0) * q_ref[m, a] + (2.0 / 3.0) * (v + TIME_STEP * rate)
            dst[m, a] = new
            if s + 1 < SECTIONS:
                put_ends(s + 1, m, a, new)

        strain = jnp.zeros((radial, cells), jnp.float32)
        held = []
        for m in (1, 2, 3):
            v, d_ax, d_rad, d_circ, lap, adv = terms(m)
            strain = strain + (d_ax * d_ax + d_rad * d_rad + d_circ * d_circ)
            held.append((m, v, lap, adv))
        nu = SMAG_COEF * jnp.sqrt(0.25 * strain + 1.0)
        for m, v, lap, adv in held:
            finish(m, v, lap, adv, nu)
        for m in (0, *range(4, comps)):
            v, _, _, _, lap, adv = terms(m)
            finish(m, v, lap, adv, nu)

    def inside(s, first, last):
        src = fields[s]

        def body(a, carry):
            update(s, a, lambda m: src[m, a - 1], lambda m: src[m, a + 1])
            return carry

        lax.fori_loop(first, last, body, 0)

    barrier = pltpu.get_barrier_semaphore()
    for side in (left, right):
        pl.semaphore_signal(
            barrier, inc=1, device_id={"row": row, "circ": side}, device_id_type=pl.DeviceIdType.MESH
        )
    for face in (0, 1):
        @pl.when(has[face])
        def _():
            for d in range(half):
                pl.semaphore_signal(
                    barrier, inc=1, device_id={"row": other_row[face], "circ": away(d)},
                    device_id_type=pl.DeviceIdType.MESH,
                )

    pack[...] = jnp.zeros_like(pack)

    def first_ends(a, carry):
        for m in range(comps):
            put_ends(0, m, a, q_ref[m, a])
        return carry

    lax.fori_loop(0, planes, first_ends, 0)
    pl.semaphore_wait(barrier, 2 + half * (has[0].astype(jnp.int32) + has[1].astype(jnp.int32)))

    cuts = [1 + (planes - 2) * i // half for i in range(half + 1)]
    for s in range(SECTIONS):
        src = fields[s]
        if s == 0:
            send_face(s, 0)
            send_face(s, 1)
        send_halo(s)
        build_select(s)
        for side in (0, 1):
            halo_copy(s, side).wait_recv()
        for m in range(comps):
            comb[m] = jnp.where(jnp.bitwise_and(lane8, 1) == 0, halo[s, 1, m], halo[s, 0, m])
        for i, d in enumerate(order):
            forward(s, d)
            if cuts[i] < cuts[i + 1]:
                inside(s, cuts[i], cuts[i + 1])
        for face in (0, 1):
            @pl.when(has[face])
            def _():
                for d in order:
                    arrival(s, face, across(d)).wait_recv()
            make_ghost(s, face)
            if face == 0:
                update(s, 0, lambda m: ghost[0, m], lambda m: src[m, 1])
            else:
                update(s, planes - 1, lambda m: src[m, planes - 2], lambda m: ghost[1, m])
            if s + 1 < SECTIONS:
                send_face(s + 1, 1 - face)

    for s in range(SECTIONS):
        for side in (0, 1):
            halo_copy(s, side).wait_send()
        for face in (0, 1):
            @pl.when(has[1 - face])
            def _():
                for d in order:
                    face_copy(s, face, d).wait_send()

            @pl.when(has[face])
            def _():
                for d in order:
                    forward_copy(s, face, d).wait_send()


def local(flow_state, velocity, offsets, passage_shift, donor_step, donor_weight):
    rows, count = lax.axis_size("row"), lax.axis_size("circ")
    comps, planes, radial, cells = flow_state.shape
    assert cells == LANES and 2 * planes * (radial // GROUP) == LANES
    vmem = pl.BlockSpec(memory_space=pltpu.VMEM)
    smem = pl.BlockSpec(memory_space=pltpu.SMEM)
    half = count // 2
    return pl.pallas_call(
        functools.partial(kernel, rows, count),
        out_shape=jax.ShapeDtypeStruct(flow_state.shape, flow_state.dtype),
        in_specs=[vmem, vmem, smem, smem, vmem, vmem],
        out_specs=vmem,
        scratch_shapes=[
            pltpu.VMEM(flow_state.shape, jnp.float32),
            pltpu.VMEM(flow_state.shape, jnp.float32),
            pltpu.VMEM((SECTIONS, comps, GROUP, cells), jnp.float32),
            pltpu.VMEM((SECTIONS, 2, comps, GROUP, cells), jnp.float32),
            pltpu.VMEM((comps, GROUP, cells), jnp.float32),
            pltpu.VMEM((2, 3 * cells, 2 * cells), jnp.bfloat16),
            pltpu.VMEM((2, comps, radial, cells), jnp.float32),
            pltpu.SemaphoreType.DMA((SECTIONS, 2, half)),
            pltpu.SemaphoreType.DMA((SECTIONS, 2, half)),
            pltpu.SemaphoreType.DMA((SECTIONS, 2, count)),
            pltpu.SemaphoreType.DMA((SECTIONS, 2)),
            pltpu.SemaphoreType.DMA((SECTIONS, 2)),
        ]
        + [pltpu.VMEM((count, comps, radial, cells), jnp.float32)] * (2 * SECTIONS),
        compiler_params=pltpu.CompilerParams(
            collective_id=0, has_side_effects=True, vmem_limit_bytes=44 * 1024 * 1024
        ),
    )(flow_state, velocity, offsets, passage_shift, donor_step, donor_weight)


def solution(mesh):
    placed = (
        P(None, "row", None, "circ"),
        P(None, "row", None, "circ"),
        P(),
        P(),
        P("row", None, "circ"),
        P("row", None, "circ"),
    )
    return jax.shard_map(
        local, mesh=mesh, in_specs=placed, out_specs=P(None, "row", None, "circ"), check_vma=False
    )
```

time: 398 us -> 73 us (0.18)
  the two profiles are of different devices: /device:TPU:2 before, /device:TPU:10 now
where the time goes in v1:
time: 73 us; the launch traced here: 72.7 us
  Pallas kernels  66.5 us (91%)
  local copies, waits for them, and re-layouts  6.2 us (8%)
    pallas_call x1, Pallas kernels, local(): pl.pallas_call(functools.partial(kernel, rows, count), out_shape=jax.Shap...  66.5 us
    unnamed x13, local copies, waits for them, and re-layouts  6.2 us

profile of v1, /device:TPU:10, one launch (start us, length us, event | category | flops | bytes accessed | tf_op | source)
XLA Modules:
  0.0 72.7 jit_solution(15674905917522074279)
XLA Ops:
  0.0 0.0 copy-start
  0.0 1.3 %copy-done = f32[5,16,32,128]{3,2,1,0:T(8,128)S(1)} copy-done((f32[5,16,32,128]{3,2,1,0:T(8,128)S(1)}, f32[5,16,32,128]{3,2,1,0:T(8,128)}, u32[]{:S(2)}) %copy-start) | copy-done | bytes 1310744
  1.3 0.0 copy-start.1
  1.3 1.1 %copy-done.1 = f32[3,16,32,128]{3,2,1,0:T(8,128)S(1)} copy-done((f32[3,16,32,128]{3,2,1,0:T(8,128)S(1)}, f32[3,16,32,128]{3,2,1,0:T(8,128)}, u32[]{:S(2)}) %copy-start.1) | copy-done | bytes 786456
  2.5 0.0 copy-start.2
  2.5 0.7 copy-done.2
  3.1 0.0 copy-start.3
  3.1 0.7 copy-done.3
  3.8 0.0 copy-start.4
  3.8 0.7 copy-done.4
  4.5 0.0 copy-start.5
  4.5 0.7 copy-done.5
  5.1 66.5 %shard_map.64 = f32[5,16,32,128]{3,2,1,0:T(8,128)S(1)} custom-call(f32[5,16,32,128]{3,2,1,0:T(8,128)S(1)} %copy-done, f32[3,16,32,128]{3,2,1,0:T(8,128)S(1)} %copy-done.1, s32[3,3]{1,0:T(4,128)S(1)} %copy-done.2, s32[4]{0:T(128)S(1)} %copy-done.5, s32[1,2,128]{2,1,0:T(2,128)S(1)} %copy-done.3, f32[1,2,128]{2,1,0:T(2,128)S(1)} %copy-done.4), custom_call_target="tpu_custom_call" | custom-call | tf_op jit(solution)/shard_map/pallas_call | solution.py:291
  71.7 1.1 %copy.8 = f32[5,16,32,128]{3,2,1,0:T(8,128)} copy(f32[5,16,32,128]{3,2,1,0:T(8,128)S(1)} %shard_map.64) | data formatting | bytes 2621440
Async XLA Ops:
  0.0 1.3 %copy-start = (f32[5,16,32,128]{3,2,1,0:T(8,128)S(1)}, f32[5,16,32,128]{3,2,1,0:T(8,128)}, u32[]{:S(2)}) copy-start(f32[5,16,32,128]{3,2,1,0:T(8,128)} %q_ref.1) | copy-start | bytes 3932164
  1.3 1.1 %copy-start.1 = (f32[3,16,32,128]{3,2,1,0:T(8,128)S(1)}, f32[3,16,32,128]{3,2,1,0:T(8,128)}, u32[]{:S(2)}) copy-start(f32[3,16,32,128]{3,2,1,0:T(8,128)} %u_ref.1) | copy-start | bytes 2359300
  2.5 0.7 copy-start.2
  3.1 0.7 copy-start.3
  3.8 0.7 copy-start.4
  4.5 0.7 copy-start.5

commit v2 on v1

--- a/solution.py
+++ b/solution.py
@@ -16,9 +16,11 @@
 
 def kernel(
     row_count, count,
-    q_ref, u_ref, off_ref, shift_ref, step_ref, weight_ref, out_ref,
-    v1, v2, pack, halo, comb, sel, ghost,
-    send_sem, fwd_sem, recv_sem, halo_send, halo_recv, *slots
+    q_in, u_in, off_in, shift_in, step_in, weight_in, out_ref,
+    q_ref, u_ref, off_ref, shift_ref, step_ref, weight_ref,
+    v1, v2, v3, pack, halo, comb, sel, ghost, share, shared, their_step, their_weight,
+    send_sem, recv_sem, share_send, share_recv, halo_send, halo_recv, load_sem, store_sem, donor_send, donor_recv,
+    *slots
 ):
     comps, planes, radial, cells = q_ref.shape
     groups = radial // GROUP
@@ -32,7 +34,7 @@
     left = lax.rem(col + count - 1, count)
     has = (row > 0, row < row_count - 1)
     other_row = (row - 1, row + 1)
-    fields = (q_ref, v1, v2, out_ref)
+    fields = (q_ref, v1, v2, v3)
     order = sorted(range(half), key=lambda d: (min(d, half - d), d))
 
     lane = lax.broadcasted_iota(jnp.int32, (radial, cells), 1)
@@ -47,26 +49,23 @@
     def back(d):
         return lax.rem(col + count - 2 * d, count)
 
-    def across(d):
-        return lax.rem(partner + count - 2 * d, count)
-
     def face_copy(s, face, d):
         plane = planes - 1 if face == 0 else 0
         return pltpu.make_async_remote_copy(
-            src_ref=fields[s].at[:, plane],
-            dst_ref=slots[2 * s + face].at[col],
+            src_ref=(q_in if s == 0 else fields[s]).at[:, plane],
+            dst_ref=slots[2 * s + face].at[col // 2],
             send_sem=send_sem.at[s, face, d],
-            recv_sem=recv_sem.at[s, face, col],
+            recv_sem=recv_sem.at[s, face, col // 2],
             device_id={"row": other_row[1 - face], "circ": away(d)},
             device_id_type=pl.DeviceIdType.MESH,
         )
 
-    def forward_copy(s, face, d):
-        return pltpu.make_async_remote_copy(
-            src_ref=slots[2 * s + face].at[back(d)],
-            dst_ref=slots[2 * s + face].at[back(d)],
-            send_sem=fwd_sem.at[s, face, d],
-            recv_sem=recv_sem.at[s, face, back(d)],
+    def share_copy(s, face):
+        return pltpu.make_async_remote_copy(
+            src_ref=share.at[s, face],
+            dst_ref=shared.at[s, face],
+            send_sem=share_send.at[s, face],
+            recv_sem=share_recv.at[s, face],
             device_id={"row": row, "circ": partner},
             device_id_type=pl.DeviceIdType.MESH,
         )
@@ -75,8 +74,18 @@
         return pltpu.make_async_remote_copy(
             src_ref=slots[2 * s + face].at[slot],
             dst_ref=slots[2 * s + face].at[slot],
-            send_sem=fwd_sem.at[s, face, 0],
+            send_sem=share_send.at[s, face],
             recv_sem=recv_sem.at[s, face, slot],
+            device_id={"row": row, "circ": partner},
+            device_id_type=pl.DeviceIdType.MESH,
+        )
+
+    def donor_copy(k):
+        return pltpu.make_async_remote_copy(
+            src_ref=(step_in, weight_in)[k],
+            dst_ref=(their_step, their_weight)[k],
+            send_sem=donor_send.at[k],
+            recv_sem=donor_recv.at[k],
             device_id={"row": row, "circ": partner},
             device_id_type=pl.DeviceIdType.MESH,
         )
@@ -100,13 +109,6 @@
     def send_halo(s):
         halo_copy(s, 0).start()
         halo_copy(s, 1).start()
-
-    def forward(s, d):
-        for face in (0, 1):
-            @pl.when(has[face])
-            def _():
-                arrival(s, face, back(d)).wait_recv()
-                forward_copy(s, face, d).start()
 
     def put_ends(s, m, a, value):
         packed = pack[s, m]
@@ -122,35 +124,56 @@
         at = jnp.clip(row - 1 + face, 0, row_count - 2)
         offset = off_ref[s, at]
         offset = offset if face == 0 else lax.rem(loop_cells - offset, loop_cells)
-        passage = col - shift_ref[row] + shift_ref[source] + offset // cells + 2 * count
-        return passage, lax.rem(offset, cells)
+        hop = lax.rem(shift_ref[source] - shift_ref[row] + offset // cells + count, count)
+        first = col - odd + hop + lax.rem(odd + hop, 2)
+        return hop, lax.rem(offset, cells), first
 
     def build_select(s):
-        spots = lax.broadcasted_iota(jnp.int32, (3 * cells, cells), 0)
+        spots = lax.broadcasted_iota(jnp.int32, (cells, cells), 0)
         within = lax.broadcasted_iota(jnp.int32, (1, cells), 1)
         for face in (0, 1):
-            _, start = donor_base(s, face)
-            donor = within + start + step_ref[0, face:face + 1, :]
-            for nxt in (0, 1):
-                hot = jnp.where(spots == donor + nxt, 1.0, 0.0).astype(jnp.bfloat16)
-                sel[face, :, nxt * cells:(nxt + 1) * cells] = hot
+            hop, start, first = donor_base(s, face)
+            for which, (who, steps) in enumerate(((col, step_ref), (partner, their_step))):
+                donor = within + start + steps[0, face:face + 1, :]
+                for k in (0, 1):
+                    place = lax.rem(first + 2 * k - who - hop + 2 * count, count) * cells
+                    for nxt in (0, 1):
+                        hot = jnp.where(spots == donor + (nxt - place), 1.0, 0.0).astype(jnp.bfloat16)
+                        at = (2 * which + nxt) * cells
+                        sel[face, k * cells:(k + 1) * cells, at:at + cells] = hot
+
+    def make_share(s, face):
+        @pl.when(has[face])
+        def _():
+            for d in order:
+                arrival(s, face, back(d) // 2).wait_recv()
+            _, _, first = donor_base(s, face)
+            base = first // 2
+            blocks = [
+                slots[2 * s + face][lax.rem(base + k, half)].reshape(comps * radial, cells) for k in (0, 1)
+            ]
+            block = jnp.concatenate(blocks, axis=1)
+            high = block.astype(jnp.bfloat16)
+            low = (block - high.astype(jnp.float32)).astype(jnp.bfloat16)
+
+            def picked(which, weights):
+                part = sel[face, :, 2 * which * cells:2 * (which + 1) * cells]
+                total = jnp.dot(high, part, preferred_element_type=jnp.float32) + jnp.dot(
+                    low, part, preferred_element_type=jnp.float32
+                )
+                weight = weights[0, face:face + 1, :]
+                value = weight * total[:, :cells] + (1.0 - weight) * total[:, cells:]
+                return value.reshape(comps, radial, cells)
+
+            share[s, face] = picked(1, their_weight)
+            share_copy(s, face).start()
+            ghost[face] = picked(0, weight_ref)
 
     def make_ghost(s, face):
         @pl.when(has[face])
         def _():
-            passage, _ = donor_base(s, face)
-            total = None
-            for k in range(3):
-                block = slots[2 * s + face][lax.rem(passage + k, count)].reshape(comps * radial, cells)
-                high = block.astype(jnp.bfloat16)
-                low = (block - high.astype(jnp.float32)).astype(jnp.bfloat16)
-                part = sel[face, k * cells:(k + 1) * cells, :]
-                for piece in (high, low):
-                    got = jnp.dot(piece, part, preferred_element_type=jnp.float32)
-                    total = got if total is None else total + got
-            weight = weight_ref[0, face:face + 1, :]
-            value = weight * total[:, :cells] + (1.0 - weight) * total[:, cells:]
-            ghost[face] = value.reshape(comps, radial, cells)
+            share_copy(s, face).wait_recv()
+            ghost[face] = ghost[face] + shared[s, face]
 
         @pl.when(jnp.logical_not(has[face]))
         def _():
@@ -227,7 +250,23 @@
                     device_id_type=pl.DeviceIdType.MESH,
                 )
 
+    loads = [
+        pltpu.make_async_copy(source, target, load_sem.at[k])
+        for k, (source, target) in enumerate((
+            (q_in, q_ref), (u_in, u_ref), (off_in, off_ref), (shift_in, shift_ref),
+            (step_in, step_ref), (weight_in, weight_ref),
+        ))
+    ]
+    for load in loads:
+        load.start()
     pack[...] = jnp.zeros_like(pack)
+    pl.semaphore_wait(barrier, 2 + half * (has[0].astype(jnp.int32) + has[1].astype(jnp.int32)))
+    send_face(0, 0)
+    send_face(0, 1)
+    for k in (0, 1):
+        donor_copy(k).start()
+    for load in loads:
+        load.wait()
 
     def first_ends(a, carry):
         for m in range(comps):
@@ -235,29 +274,29 @@
         return carry
 
     lax.fori_loop(0, planes, first_ends, 0)
-    pl.semaphore_wait(barrier, 2 + half * (has[0].astype(jnp.int32) + has[1].astype(jnp.int32)))
-
-    cuts = [1 + (planes - 2) * i // half for i in range(half + 1)]
+    for k in (0, 1):
+        donor_copy(k).wait_recv()
+
+    middle = max(1, planes * 5 // 8)
+    stores = [
+        pltpu.make_async_copy(v3.at[:, a:b], out_ref.at[:, a:b], store_sem.at[k])
+        for k, (a, b) in enumerate(((1, planes - 1), (0, 1), (planes - 1, planes)))
+    ]
     for s in range(SECTIONS):
         src = fields[s]
-        if s == 0:
-            send_face(s, 0)
-            send_face(s, 1)
         send_halo(s)
         build_select(s)
         for side in (0, 1):
             halo_copy(s, side).wait_recv()
         for m in range(comps):
             comb[m] = jnp.where(jnp.bitwise_and(lane8, 1) == 0, halo[s, 1, m], halo[s, 0, m])
-        for i, d in enumerate(order):
-            forward(s, d)
-            if cuts[i] < cuts[i + 1]:
-                inside(s, cuts[i], cuts[i + 1])
+        inside(s, 1, middle)
         for face in (0, 1):
-            @pl.when(has[face])
-            def _():
-                for d in order:
-                    arrival(s, face, across(d)).wait_recv()
+            make_share(s, face)
+        inside(s, middle, planes - 1)
+        if s + 1 == SECTIONS:
+            stores[0].start()
+        for face in (0, 1):
             make_ghost(s, face)
             if face == 0:
                 update(s, 0, lambda m: ghost[0, m], lambda m: src[m, 1])
@@ -265,7 +304,13 @@
                 update(s, planes - 1, lambda m: src[m, planes - 2], lambda m: ghost[1, m])
             if s + 1 < SECTIONS:
                 send_face(s + 1, 1 - face)
-
+            else:
+                stores[1 + face].start()
+
+    for store in stores:
+        store.wait()
+    for k in (0, 1):
+        donor_copy(k).wait_send()
     for s in range(SECTIONS):
         for side in (0, 1):
             halo_copy(s, side).wait_send()
@@ -277,37 +322,52 @@
 
             @pl.when(has[face])
             def _():
-                for d in order:
-                    forward_copy(s, face, d).wait_send()
+                share_copy(s, face).wait_send()
 
 
 def local(flow_state, velocity, offsets, passage_shift, donor_step, donor_weight):
     rows, count = lax.axis_size("row"), lax.axis_size("circ")
     comps, planes, radial, cells = flow_state.shape
     assert cells == LANES and 2 * planes * (radial // GROUP) == LANES
-    vmem = pl.BlockSpec(memory_space=pltpu.VMEM)
-    smem = pl.BlockSpec(memory_space=pltpu.SMEM)
+    whole = pl.BlockSpec(memory_space=pl.ANY)
     half = count // 2
+    face = (comps, radial, cells)
     return pl.pallas_call(
         functools.partial(kernel, rows, count),
         out_shape=jax.ShapeDtypeStruct(flow_state.shape, flow_state.dtype),
-        in_specs=[vmem, vmem, smem, smem, vmem, vmem],
-        out_specs=vmem,
+        in_specs=[whole] * 6,
+        out_specs=whole,
         scratch_shapes=[
+            pltpu.VMEM(flow_state.shape, jnp.float32),
+            pltpu.VMEM(velocity.shape, jnp.float32),
+            pltpu.SMEM(offsets.shape, jnp.int32),
+            pltpu.SMEM(passage_shift.shape, jnp.int32),
+            pltpu.VMEM(donor_step.shape, jnp.int32),
+            pltpu.VMEM(donor_weight.shape, jnp.float32),
+            pltpu.VMEM(flow_state.shape, jnp.float32),
             pltpu.VMEM(flow_state.shape, jnp.float32),
             pltpu.VMEM(flow_state.shape, jnp.float32),
             pltpu.VMEM((SECTIONS, comps, GROUP, cells), jnp.float32),
             pltpu.VMEM((SECTIONS, 2, comps, GROUP, cells), jnp.float32),
             pltpu.VMEM((comps, GROUP, cells), jnp.float32),
-            pltpu.VMEM((2, 3 * cells, 2 * cells), jnp.bfloat16),
-            pltpu.VMEM((2, comps, radial, cells), jnp.float32),
+            pltpu.VMEM((2, 2 * cells, 4 * cells), jnp.bfloat16),
+            pltpu.VMEM((2, *face), jnp.float32),
+            pltpu.VMEM((SECTIONS, 2, *face), jnp.float32),
+            pltpu.VMEM((SECTIONS, 2, *face), jnp.float32),
+            pltpu.VMEM(donor_step.shape, jnp.int32),
+            pltpu.VMEM(donor_weight.shape, jnp.float32),
             pltpu.SemaphoreType.DMA((SECTIONS, 2, half)),
             pltpu.SemaphoreType.DMA((SECTIONS, 2, half)),
-            pltpu.SemaphoreType.DMA((SECTIONS, 2, count)),
             pltpu.SemaphoreType.DMA((SECTIONS, 2)),
             pltpu.SemaphoreType.DMA((SECTIONS, 2)),
+            pltpu.SemaphoreType.DMA((SECTIONS, 2)),
+            pltpu.SemaphoreType.DMA((SECTIONS, 2)),
+            pltpu.SemaphoreType.DMA((6,)),
+            pltpu.SemaphoreType.DMA((3,)),
+            pltpu.SemaphoreType.DMA((2,)),
+            pltpu.SemaphoreType.DMA((2,)),
         ]
-        + [pltpu.VMEM((count, comps, radial, cells), jnp.float32)] * (2 * SECTIONS),
+        + [pltpu.VMEM((half, *face), jnp.float32)] * (2 * SECTIONS),
         compiler_params=pltpu.CompilerParams(
             collective_id=0, has_side_effects=True, vmem_limit_bytes=44 * 1024 * 1024
         ),

time: 73 us -> 62.5 us (0.86)
  the two profiles are of different devices: /device:TPU:10 before, /device:TPU:2 now
where the time goes in v2:
time: 62.5 us; the launch traced here: 61.2 us
  Pallas kernels  55 us (88%)
  local copies, waits for them, and re-layouts  6.2 us (10%)
    pallas_call x1, Pallas kernels, local(): pl.pallas_call(functools.partial(kernel, rows, count), out_shape=jax.Shap...  55 us
    unnamed x13, local copies, waits for them, and re-layouts  6.2 us

profile of v2, /device:TPU:2, one launch (start us, length us, event | category | flops | bytes accessed | tf_op | source)
XLA Modules:
  0.0 61.2 jit_solution(821709544572805201)
XLA Ops:
  0.0 0.0 copy-start
  0.0 1.3 %copy-done = f32[5,16,32,128]{3,2,1,0:T(8,128)S(1)} copy-done((f32[5,16,32,128]{3,2,1,0:T(8,128)S(1)}, f32[5,16,32,128]{3,2,1,0:T(8,128)}, u32[]{:S(2)}) %copy-start) | copy-done | bytes 1310744
  1.3 0.0 copy-start.1
  1.3 1.1 %copy-done.1 = f32[3,16,32,128]{3,2,1,0:T(8,128)S(1)} copy-done((f32[3,16,32,128]{3,2,1,0:T(8,128)S(1)}, f32[3,16,32,128]{3,2,1,0:T(8,128)}, u32[]{:S(2)}) %copy-start.1) | copy-done | bytes 786456
  2.5 0.0 copy-start.2
  2.5 0.7 %copy-done.2 = s32[3,3]{1,0:T(4,128)S(1)} copy-done((s32[3,3]{1,0:T(4,128)S(1)}, s32[3,3]{1,0:T(4,128)}, u32[]{:S(2)}) %copy-start.2) | copy-done | bytes 60
  3.1 0.0 copy-start.3
  3.1 0.7 %copy-done.3 = s32[1,2,128]{2,1,0:T(2,128)S(1)} copy-done((s32[1,2,128]{2,1,0:T(2,128)S(1)}, s32[1,2,128]{2,1,0:T(2,128)}, u32[]{:S(2)}) %copy-start.3) | copy-done | bytes 1048
  3.8 0.0 copy-start.4
  3.8 0.7 %copy-done.4 = f32[1,2,128]{2,1,0:T(2,128)S(1)} copy-done((f32[1,2,128]{2,1,0:T(2,128)S(1)}, f32[1,2,128]{2,1,0:T(2,128)}, u32[]{:S(2)}) %copy-start.4) | copy-done | bytes 1048
  4.5 0.0 copy-start.5
  4.5 0.7 %copy-done.5 = s32[4]{0:T(128)S(1)} copy-done((s32[4]{0:T(128)S(1)}, s32[4]{0:T(128)}, u32[]{:S(2)}) %copy-start.5) | copy-done | bytes 40
  5.1 55.0 %shard_map.64 = f32[5,16,32,128]{3,2,1,0:T(8,128)S(1)} custom-call(f32[5,16,32,128]{3,2,1,0:T(8,128)S(1)} %copy-done, f32[3,16,32,128]{3,2,1,0:T(8,128)S(1)} %copy-done.1, s32[3,3]{1,0:T(4,128)S(1)} %copy-done.2, s32[4]{0:T(128)S(1)} %copy-done.5, s32[1,2,128]{2,1,0:T(2,128)S(1)} %copy-done.3, f32[1,2,128]{2,1,0:T(2,128)S(1)} %copy-done.4), custom_call_target="tpu_custom_call" | custom-call | tf_op jit(solution)/shard_map/pallas_call | solution.py:335
  60.2 1.1 %copy.8 = f32[5,16,32,128]{3,2,1,0:T(8,128)} copy(f32[5,16,32,128]{3,2,1,0:T(8,128)S(1)} %shard_map.64) | data formatting | bytes 2621440
Async XLA Ops:
  0.0 1.3 %copy-start = (f32[5,16,32,128]{3,2,1,0:T(8,128)S(1)}, f32[5,16,32,128]{3,2,1,0:T(8,128)}, u32[]{:S(2)}) copy-start(f32[5,16,32,128]{3,2,1,0:T(8,128)} %q_in.1) | copy-start | bytes 3932164
  1.3 1.1 %copy-start.1 = (f32[3,16,32,128]{3,2,1,0:T(8,128)S(1)}, f32[3,16,32,128]{3,2,1,0:T(8,128)}, u32[]{:S(2)}) copy-start(f32[3,16,32,128]{3,2,1,0:T(8,128)} %u_in.1) | copy-start | bytes 2359300
  2.5 0.7 %copy-start.2 = (s32[3,3]{1,0:T(4,128)S(1)}, s32[3,3]{1,0:T(4,128)}, u32[]{:S(2)}) copy-start(s32[3,3]{1,0:T(4,128)} %off_in.1) | copy-start | bytes 112
  3.1 0.7 %copy-start.3 = (s32[1,2,128]{2,1,0:T(2,128)S(1)}, s32[1,2,128]{2,1,0:T(2,128)}, u32[]{:S(2)}) copy-start(s32[1,2,128]{2,1,0:T(2,128)} %step_in.1) | copy-start | bytes 3076
  3.8 0.7 %copy-start.4 = (f32[1,2,128]{2,1,0:T(2,128)S(1)}, f32[1,2,128]{2,1,0:T(2,128)}, u32[]{:S(2)}) copy-start(f32[1,2,128]{2,1,0:T(2,128)} %weight_in.1) | copy-start | bytes 3076
  4.5 0.7 %copy-start.5 = (s32[4]{0:T(128)S(1)}, s32[4]{0:T(128)}, u32[]{:S(2)}) copy-start(s32[4]{0:T(128)} %shift_in.1) | copy-start | bytes 52

commit v3 on v2

--- a/solution.py
+++ b/solution.py
@@ -19,7 +19,7 @@
     q_in, u_in, off_in, shift_in, step_in, weight_in, out_ref,
     q_ref, u_ref, off_ref, shift_ref, step_ref, weight_ref,
     v1, v2, v3, pack, halo, comb, sel, ghost, share, shared, their_step, their_weight,
-    send_sem, recv_sem, share_send, share_recv, halo_send, halo_recv, load_sem, store_sem, donor_send, donor_recv,
+    send_sem, relay_send, recv_sem, share_send, share_recv, halo_send, halo_recv, load_sem, store_sem, donor_send, donor_recv,
     *slots
 ):
     comps, planes, radial, cells = q_ref.shape
@@ -35,7 +35,8 @@
     has = (row > 0, row < row_count - 1)
     other_row = (row - 1, row + 1)
     fields = (q_ref, v1, v2, v3)
-    order = sorted(range(half), key=lambda d: (min(d, half - d), d))
+    spot_in_line = col // 2
+    not_low, not_high = spot_in_line > 0, spot_in_line < half - 1
 
     lane = lax.broadcasted_iota(jnp.int32, (radial, cells), 1)
     line = lax.broadcasted_iota(jnp.int32, (radial, cells), 0)
@@ -43,20 +44,27 @@
     is_first, is_last = lane == 0, lane == cells - 1
     is_inner, is_outer = line == 0, line == radial - 1
 
-    def away(d):
-        return lax.rem(col + 2 * d, count)
-
-    def back(d):
-        return lax.rem(col + count - 2 * d, count)
-
-    def face_copy(s, face, d):
+    def reaches(step):
+        return {0: row >= 0, 1: not_high, -1: not_low}[step]
+
+    def face_copy(s, face, step):
         plane = planes - 1 if face == 0 else 0
         return pltpu.make_async_remote_copy(
             src_ref=(q_in if s == 0 else fields[s]).at[:, plane],
             dst_ref=slots[2 * s + face].at[col // 2],
-            send_sem=send_sem.at[s, face, d],
+            send_sem=send_sem.at[s, face, step + 1],
             recv_sem=recv_sem.at[s, face, col // 2],
-            device_id={"row": other_row[1 - face], "circ": away(d)},
+            device_id={"row": other_row[1 - face], "circ": col + 2 * step},
+            device_id_type=pl.DeviceIdType.MESH,
+        )
+
+    def relay_copy(s, face, slot, step):
+        return pltpu.make_async_remote_copy(
+            src_ref=slots[2 * s + face].at[slot],
+            dst_ref=slots[2 * s + face].at[slot],
+            send_sem=relay_send.at[s, face, slot],
+            recv_sem=recv_sem.at[s, face, slot],
+            device_id={"row": row, "circ": col + 2 * step},
             device_id_type=pl.DeviceIdType.MESH,
         )
 
@@ -103,8 +111,22 @@
     def send_face(s, face):
         @pl.when(has[1 - face])
         def _():
-            for d in order:
-                face_copy(s, face, d).start()
+            for step in (1, -1, 0):
+                @pl.when(reaches(step))
+                def _():
+                    face_copy(s, face, step).start()
+
+    def relay(s, distance):
+        for face in (0, 1):
+            for step in (1, -1):
+                slot = spot_in_line - step * distance
+                @pl.when(has[face] & (slot >= 0) & (slot < half))
+                def _():
+                    arrival(s, face, slot).wait_recv()
+
+                    @pl.when(reaches(step))
+                    def _():
+                        relay_copy(s, face, slot, step).start()
 
     def send_halo(s):
         halo_copy(s, 0).start()
@@ -145,8 +167,7 @@
     def make_share(s, face):
         @pl.when(has[face])
         def _():
-            for d in order:
-                arrival(s, face, back(d) // 2).wait_recv()
+            arrival(s, face, spot_in_line).wait_recv()
             _, _, first = donor_base(s, face)
             base = first // 2
             blocks = [
@@ -244,11 +265,20 @@
     for face in (0, 1):
         @pl.when(has[face])
         def _():
-            for d in range(half):
-                pl.semaphore_signal(
-                    barrier, inc=1, device_id={"row": other_row[face], "circ": away(d)},
-                    device_id_type=pl.DeviceIdType.MESH,
-                )
+            for step in (0, 1, -1):
+                @pl.when(reaches(step))
+                def _():
+                    pl.semaphore_signal(
+                        barrier, inc=1, device_id={"row": other_row[face], "circ": col + 2 * step},
+                        device_id_type=pl.DeviceIdType.MESH,
+                    )
+    for step in (1, -1):
+        @pl.when(reaches(step))
+        def _():
+            pl.semaphore_signal(
+                barrier, inc=1, device_id={"row": row, "circ": col + 2 * step},
+                device_id_type=pl.DeviceIdType.MESH,
+            )
 
     loads = [
         pltpu.make_async_copy(source, target, load_sem.at[k])
@@ -260,7 +290,10 @@
     for load in loads:
         load.start()
     pack[...] = jnp.zeros_like(pack)
-    pl.semaphore_wait(barrier, 2 + half * (has[0].astype(jnp.int32) + has[1].astype(jnp.int32)))
+    line_sides = not_low.astype(jnp.int32) + not_high.astype(jnp.int32)
+    pl.semaphore_wait(
+        barrier, 2 + line_sides + (1 + line_sides) * (has[0].astype(jnp.int32) + has[1].astype(jnp.int32))
+    )
     send_face(0, 0)
     send_face(0, 1)
     for k in (0, 1):
@@ -277,7 +310,8 @@
     for k in (0, 1):
         donor_copy(k).wait_recv()
 
-    middle = max(1, planes * 5 // 8)
+    middle = planes * 5 // 8
+    cuts = [1 + (middle - 1) * i // (half - 1) for i in range(half)]
     stores = [
         pltpu.make_async_copy(v3.at[:, a:b], out_ref.at[:, a:b], store_sem.at[k])
         for k, (a, b) in enumerate(((1, planes - 1), (0, 1), (planes - 1, planes)))
@@ -290,7 +324,10 @@
             halo_copy(s, side).wait_recv()
         for m in range(comps):
             comb[m] = jnp.where(jnp.bitwise_and(lane8, 1) == 0, halo[s, 1, m], halo[s, 0, m])
-        inside(s, 1, middle)
+        for i in range(half - 1):
+            if cuts[i] < cuts[i + 1]:
+                inside(s, cuts[i], cuts[i + 1])
+            relay(s, i + 1)
         for face in (0, 1):
             make_share(s, face)
         inside(s, middle, planes - 1)
@@ -317,12 +354,18 @@
         for face in (0, 1):
             @pl.when(has[1 - face])
             def _():
-                for d in order:
-                    face_copy(s, face, d).wait_send()
+                for step in (1, -1, 0):
+                    @pl.when(reaches(step))
+                    def _():
+                        face_copy(s, face, step).wait_send()
 
             @pl.when(has[face])
             def _():
                 share_copy(s, face).wait_send()
+                for slot in range(half):
+                    @pl.when(((spot_in_line > slot) & not_high) | ((spot_in_line < slot) & not_low))
+                    def _():
+                        relay_copy(s, face, slot, 1).wait_send()
 
 
 def local(flow_state, velocity, offsets, passage_shift, donor_step, donor_weight):
@@ -356,6 +399,7 @@
             pltpu.VMEM((SECTIONS, 2, *face), jnp.float32),
             pltpu.VMEM(donor_step.shape, jnp.int32),
             pltpu.VMEM(donor_weight.shape, jnp.float32),
+            pltpu.SemaphoreType.DMA((SECTIONS, 2, 3)),
             pltpu.SemaphoreType.DMA((SECTIONS, 2, half)),
             pltpu.SemaphoreType.DMA((SECTIONS, 2, half)),
             pltpu.SemaphoreType.DMA((SECTIONS, 2)),
@@ -369,7 +413,7 @@
         ]
         + [pltpu.VMEM((half, *face), jnp.float32)] * (2 * SECTIONS),
         compiler_params=pltpu.CompilerParams(
-            collective_id=0, has_side_effects=True, vmem_limit_bytes=44 * 1024 * 1024
+            collective_id=0, has_side_effects=True, vmem_limit_bytes=63 * 1024 * 1024
         ),
     )(flow_state, velocity, offsets, passage_shift, donor_step, donor_weight)
 

time: 62.5 us -> 61.7 us (0.987); the launches traced: 61.2 us -> 61.6 us
  Pallas kernels: 55 us -> 59 us
  local copies, waits for them, and re-layouts: 6.2 us -> 2.52 us
    pallas_call x1, Pallas kernels: 55 us -> 59 us  [local(): pl.pallas_call(functools.partial(kernel, rows, count), out_shape=jax.Shap...]
    unnamed x13 -> x1, local copies, waits for them, and re-layouts: 6.2 us -> 2.52 us
where the time goes in v3:
time: 61.7 us; the launch traced here: 61.6 us
  Pallas kernels  59 us (96%)
  local copies, waits for them, and re-layouts  2.52 us (4%)
    pallas_call x1, Pallas kernels, local(): pl.pallas_call(functools.partial(kernel, rows, count), out_shape=jax.Shap...  59 us
    unnamed x1, local copies, waits for them, and re-layouts  2.52 us

profile of v3, /device:TPU:2, one launch (start us, length us, event | category | flops | bytes accessed | tf_op | source)
XLA Modules:
  0.0 61.6 jit_solution(15867436251635616824)
XLA Ops:
  0.0 59.0 %shard_map.64 = f32[5,16,32,128]{3,2,1,0:T(8,128)} custom-call(f32[5,16,32,128]{3,2,1,0:T(8,128)} %q_in.1, f32[3,16,32,128]{3,2,1,0:T(8,128)} %u_in.1, s32[3,3]{1,0:T(4,128)} %off_in.1, s32[4]{0:T(128)} %shift_in.1, s32[1,2,128]{2,1,0:T(2,128)} %step_in.1, f32[1,2,128]{2,1,0:T(2,128)} %weight_in.1), custom_call_target="tpu_custom_call" | custom-call | tf_op jit(solution)/shard_map/pallas_call | solution.py:378
  59.0 2.5 %copy.8 = f32[5,16,32,128]{3,2,1,0:T(8,128)} copy(f32[5,16,32,128]{3,2,1,0:T(8,128)} %shard_map.64) | data formatting | bytes 2621440

commit v4 on v2

--- a/solution.py
+++ b/solution.py
@@ -369,7 +369,7 @@
         ]
         + [pltpu.VMEM((half, *face), jnp.float32)] * (2 * SECTIONS),
         compiler_params=pltpu.CompilerParams(
-            collective_id=0, has_side_effects=True, vmem_limit_bytes=44 * 1024 * 1024
+            collective_id=0, has_side_effects=True, vmem_limit_bytes=63 * 1024 * 1024
         ),
     )(flow_state, velocity, offsets, passage_shift, donor_step, donor_weight)
 

time: 62.5 us -> 59.4 us (0.950)
  local copies, waits for them, and re-layouts: 6.2 us -> 2.52 us
  Pallas kernels: 55 us -> 55.8 us
    unnamed x13 -> x1, local copies, waits for them, and re-layouts: 6.2 us -> 2.52 us
    pallas_call x1, Pallas kernels: 55 us -> 55.8 us  [local(): pl.pallas_call(functools.partial(kernel, rows, count), out_shape=jax.Shap...]
where the time goes in v4:
time: 59.4 us; the launch traced here: 58.4 us
  Pallas kernels  55.8 us (94%)
  local copies, waits for them, and re-layouts  2.52 us (4%)
    pallas_call x1, Pallas kernels, local(): pl.pallas_call(functools.partial(kernel, rows, count), out_shape=jax.Shap...  55.8 us
    unnamed x1, local copies, waits for them, and re-layouts  2.52 us

profile of v4, /device:TPU:2, one launch (start us, length us, event | category | flops | bytes accessed | tf_op | source)
XLA Modules:
  0.0 58.4 jit_solution(4048407725098770851)
XLA Ops:
  0.0 55.8 %shard_map.64 = f32[5,16,32,128]{3,2,1,0:T(8,128)} custom-call(f32[5,16,32,128]{3,2,1,0:T(8,128)} %q_in.1, f32[3,16,32,128]{3,2,1,0:T(8,128)} %u_in.1, s32[3,3]{1,0:T(4,128)} %off_in.1, s32[4]{0:T(128)} %shift_in.1, s32[1,2,128]{2,1,0:T(2,128)} %step_in.1, f32[1,2,128]{2,1,0:T(2,128)} %weight_in.1), custom_call_target="tpu_custom_call" | custom-call | tf_op jit(solution)/shard_map/pallas_call | solution.py:335
  55.8 2.5 %copy.8 = f32[5,16,32,128]{3,2,1,0:T(8,128)} copy(f32[5,16,32,128]{3,2,1,0:T(8,128)} %shard_map.64) | data formatting | bytes 2621440
